TPU v7x, 32 devices: a whole 2x2x4 slice. The times are simulated.
32 devices in a mesh: dp: 4 (over x, core), ctx: 8 (over z, y).
Axes of the slice: x: 2, y: 2, z: 4, core: 2. Of those that a mesh axis runs over, the one named last changes fastest.
Arguments:
- queries: bfloat16 [4, 1024, 2048], P('dp', 'ctx'), may hold values from -150 to 150
- key_rows: bfloat16 [4, 1024, 512], P('dp', 'ctx'), may hold values from -5 to 5
- value_rows: bfloat16 [4, 1024, 512], P('dp', 'ctx'), may hold values from -6 to 6
- cotangent: bfloat16 [4, 1024, 2048], P('dp', 'ctx'), may hold values from -6 to 6
- sink_logits: float32 [16], replicated, may hold values from -1 to 3
- run_lengths: int32 [4, 3], P('dp'), may hold values from 1 to 4, 8 in all within a row
- segment_ids: int32 [4, 1024], P('dp', 'ctx'), may hold values from 0 to 3, never falling along the last dimension, each value on 1 to 512 neighbouring positions
Outputs:
- attended: bfloat16 [4, 1024, 2048], P('dp', 'ctx')
- grad_queries: bfloat16 [4, 1024, 2048], P('dp', 'ctx')
- grad_keys: bfloat16 [4, 1024, 512], P('dp', 'ctx')
- grad_values: bfloat16 [4, 1024, 512], P('dp', 'ctx')
- grad_sink: float32 [16], replicated
Inputs may be any that keep to these rules, and one draw needn't show every extreme that they name: `run_lengths`: in each sequence the trajectories cover all shards in order; each spans 1 to 4 shards and one spans exactly 4. `segment_ids`: never falls along a sequence; each episode spans 1 to 512 tokens and one spans exactly 512.
All inputs are finite; a program needn't handle non-finite values.
Results may differ from a plain program's by a relative error of at most 0.04.
Values may be sent and summed in bfloat16 or wider, within the bound.
A program may use at most 64 MiB of HBM per device.

v0:
```python
import math

import jax
import jax.numpy as jnp
from jax import lax
from jax.sharding import PartitionSpec as P

HEADS = 16
KV_HEADS = 4
HEAD_DIM = 128


def shortened(array):

    def short(part):
        return part.astype(jnp.bfloat16) if part.dtype == jnp.float32 else part

    return jax.tree.map(short, array)


def passed_along(array, axis, by):
    devices = lax.axis_size(axis)
    pairs = [(i, i + by) for i in range(devices) if 0 <= i + by < devices]
    return lax.ppermute(array, axis, pairs)


def traj_index(run_ends, shard_index):
    return jnp.sum((run_ends[None, :] <= shard_index[:, None]).astype(jnp.int32), axis=1)


def head_block(query_heads, key_win, value_win, grad_heads, allowed, sink_part, factor):
    scores = (
        jnp.einsum("rgd,wd->grw", query_heads, key_win, preferred_element_type=jnp.float32) * factor
    )
    scores = jnp.where(allowed[None], scores, -jnp.inf)
    row_top = jnp.maximum(jnp.max(scores, axis=2), sink_part[:, None])
    exp_terms = jnp.exp(scores - row_top[:, :, None])
    sink_exp = jnp.exp(sink_part[:, None] - row_top)
    denominator = jnp.sum(exp_terms, axis=2) + sink_exp
    weights = exp_terms / denominator[:, :, None]
    weights_low = weights.astype(jnp.bfloat16)
    attended = jnp.einsum(
        "grw,wd->rgd", weights_low, value_win, preferred_element_type=jnp.float32
    ).astype(jnp.bfloat16)
    row_dot = jnp.sum(grad_heads.astype(jnp.float32) * attended.astype(jnp.float32), axis=2).T
    grad_weights = jnp.einsum(
        "rgd,wd->grw", grad_heads, value_win, preferred_element_type=jnp.float32
    )
    grad_scores = (weights * (grad_weights - row_dot[:, :, None])).astype(jnp.bfloat16)
    grad_query = (
        jnp.einsum("grw,wd->rgd", grad_scores, key_win, preferred_element_type=jnp.float32) * factor
    ).astype(jnp.bfloat16)
    grad_key = (
        jnp.einsum("grw,rgd->wd", grad_scores, query_heads, preferred_element_type=jnp.float32)
        * factor
    )
    grad_value = jnp.einsum(
        "grw,rgd->wd", weights_low, grad_heads, preferred_element_type=jnp.float32
    )
    grad_sink = -jnp.sum(sink_exp / denominator * row_dot, axis=1)
    return (attended, grad_query, grad_key, grad_value, grad_sink)


def body(queries, key_rows, value_rows, cotangent, sink_logits, run_lengths, segment_ids):
    tok_rows = queries.shape[1]
    n_ctx = lax.axis_size("ctx")
    most_shards = min(8, n_ctx // 2)
    ctx_index = lax.axis_index("ctx")
    group_size = HEADS // KV_HEADS
    factor = HEAD_DIM ** (-0.5)
    query_loc = queries[0]
    key_loc = key_rows[0]
    value_loc = value_rows[0]
    grad_loc = cotangent[0]
    seg_mark = segment_ids[0].astype(jnp.bfloat16)
    lengths = run_lengths[0]
    run_ends = jnp.cumsum(lengths)
    own_shard = (key_loc, value_loc, seg_mark)
    gathered = own_shard
    width_now = 1
    while width_now < most_shards:
        arrived = jax.tree.map(
            lambda part, own: part.astype(own.dtype),
            passed_along(shortened(gathered), "ctx", width_now),
            gathered,
        )
        kept_width = min(2 * width_now, most_shards)
        start_row = (2 * width_now - kept_width) * tok_rows
        gathered = tuple(
            (
                jnp.concatenate([fresh_rows, older_rows], 0)
                for fresh_rows, older_rows in zip(arrived, gathered)
            )
        )
        width_now = kept_width
    key_win, value_win, seg_win = gathered
    my_traj = traj_index(run_ends, ctx_index[None])[0]
    query_pos = ctx_index * tok_rows + jnp.arange(tok_rows, dtype=jnp.int32)

    def window_work(width):
        first_col = (most_shards - width) * tok_rows
        columns = jnp.arange(width * tok_rows, dtype=jnp.int32)
        key_shard = ctx_index - width + 1 + columns // tok_rows
        key_pos = key_shard * tok_rows + columns % tok_rows
        allowed = (
            ((key_shard >= 0) & (traj_index(run_ends, key_shard) == my_traj))[None, :]
            & (seg_win[None, :] == seg_mark[:, None])
            & (key_pos[None, :] <= query_pos[:, None])
        )
        outs_list = [[], [], [], [], []]
        for kv_head in range(KV_HEADS):
            query_cols = slice(
                kv_head * group_size * HEAD_DIM, (kv_head + 1) * group_size * HEAD_DIM
            )
            key_cols = slice(kv_head * HEAD_DIM, (kv_head + 1) * HEAD_DIM)
            head_parts = head_block(
                query_loc[:, query_cols].reshape(tok_rows, group_size, HEAD_DIM),
                key_win[first_col:, key_cols],
                value_win[first_col:, key_cols],
                grad_loc[:, query_cols].reshape(tok_rows, group_size, HEAD_DIM),
                allowed,
                sink_logits[kv_head * group_size : (kv_head + 1) * group_size],
                factor,
            )
            for member in range(5):
                outs_list[member].append(head_parts[member])
        front_pad = ((first_col, 0), (0, 0))
        attended = jnp.concatenate(
            [block_out.reshape(tok_rows, -1) for block_out in outs_list[0]], 1
        )
        grad_query = jnp.concatenate(
            [block_out.reshape(tok_rows, -1) for block_out in outs_list[1]], 1
        )
        grad_key = jnp.concatenate(outs_list[2], 1)
        grad_value = jnp.concatenate(outs_list[3], 1)
        grad_sink = jnp.concatenate(outs_list[4], 0)
        return (attended, grad_query, grad_key, grad_value, grad_sink)

    attended, grad_query, grad_key, grad_value, grad_sink = window_work(most_shards)
    width_list = [1]
    while width_list[-1] < most_shards:
        width_list.append(min(2 * width_list[-1], most_shards))
    carried = (grad_key, grad_value)
    for section in range(len(width_list) - 1, 0, -1):
        kept_width = width_list[section]
        width_now = width_list[section - 1]
        front_rows = (2 * width_now - kept_width) * tok_rows
        padded = tuple((member_rows for member_rows in carried))
        split_row = width_now * tok_rows
        returned = passed_along(
            (
                padded[0][:split_row].astype(jnp.bfloat16),
                padded[1][:split_row].astype(jnp.bfloat16),
            ),
            "ctx",
            -width_now,
        )
        carried = (
            padded[0][split_row:] + returned[0].astype(jnp.float32),
            padded[1][split_row:] + returned[1].astype(jnp.float32),
        )
    sink_total = lax.psum(grad_sink, ("dp", "ctx"))
    scale_down = 1.0 / math.sqrt(lax.axis_size("dp") * n_ctx * tok_rows)
    return (
        attended[None],
        grad_query[None],
        carried[0].astype(jnp.bfloat16)[None],
        carried[1].astype(jnp.bfloat16)[None],
        sink_total * scale_down,
    )


def solution(mesh):
    in_specs = (
        P("dp", "ctx", None),
        P("dp", "ctx", None),
        P("dp", "ctx", None),
        P("dp", "ctx", None),
        P(),
        P("dp", None),
        P("dp", "ctx"),
    )
    out_specs = (
        P("dp", "ctx", None),
        P("dp", "ctx", None),
        P("dp", "ctx", None),
        P("dp", "ctx", None),
        P(),
    )
    return jax.shard_map(body, mesh=mesh, in_specs=in_specs, out_specs=out_specs, check_vma=False)
```

profile of v0, /device:TPU:0, one launch (start us, length us, event | category | flops | bytes accessed | tf_op | source)
XLA Modules:
  0.0 111.3 jit_solution(9066264888493731365)
XLA Ops:
  1.3 5.0 %collective-permute-start.2 = (bf16[128]{0:T(256)(128)(2,1)S(1)}, bf16[128]{0:T(256)(128)(2,1)S(1)}, u32[]{:S(2)}, u32[]{:S(2)}) collective-permute-start(bf16[128]{0:T(256)(128)(2,1)S(1)} %convert_bitcast_fusion), channel_id=1, source_target_pairs={{0,1},{1,2},{2,3},{3,4},{4,5},{5,6},{6,7},{8,9},{9,10},{10,11},{11... | collective-permute-start | bytes 776 | tf_op jit(solution)/shard_map/ppermute | solution.py:24
  6.3 1.0 copy.107
  7.3 3.4 %collective-permute-start = (bf16[128,512]{0,1:T(8,128)(2,1)S(1)}, bf16[128,512]{0,1:T(8,128)(2,1)S(1)}, u32[]{:S(2)}, u32[]{:S(2)}) collective-permute-start(bf16[128,512]{0,1:T(8,128)(2,1)S(1)} %bitcast.233), channel_id=1, source_target_pairs={{0,1},{1,2},{2,3},{3,4},{4,5},{5,6},{6,7},{8,9},{9,10},{10,11},{11... | collective-permute-start | bytes 393224 | tf_op jit(solution)/shard_map/ppermute | solution.py:24
  10.8 3.4 %collective-permute-start.4 = (bf16[128,512]{1,0:T(8,128)(2,1)S(1)}, bf16[128,512]{1,0:T(8,128)(2,1)S(1)}, u32[]{:S(2)}, u32[]{:S(2)}) collective-permute-start(bf16[128,512]{1,0:T(8,128)(2,1)S(1)} %bitcast.253), channel_id=1, source_target_pairs={{0,1},{1,2},{2,3},{3,4},{4,5},{5,6},{6,7},{8,9},{9,10},{10,11},{11... | collective-permute-start | bytes 393224 | tf_op jit(solution)/shard_map/ppermute | solution.py:24
  15.8 1.3 %copy.108 = bf16[1,128,2048]{1,2,0:T(8,128)(2,1)S(1)} copy(bf16[1,128,2048]{2,1,0:T(8,128)(2,1)} %param.7) | data formatting | bytes 1048576 | tf_op args[0]
  17.2 1.0 copy-done.7
  19.0 3.5 %collective-permute-start.3 = (bf16[256]{0:T(256)(128)(2,1)S(1)}, bf16[256]{0:T(256)(128)(2,1)S(1)}, u32[]{:S(2)}, u32[]{:S(2)}) collective-permute-start(bf16[256]{0:T(256)(128)(2,1)S(1)} %pad_maximum_fusion.7), channel_id=1, source_target_pairs={{0,2},{1,3},{2,4},{3,5},{4,6},{5,7},{8,10},{9,11},{10,12},{11,13},... | collective-permute-start | bytes 1544 | tf_op jit(solution)/shard_map/ppermute | solution.py:24
  23.8 4.2 %collective-permute-start.5 = (bf16[256,512]{1,0:T(8,128)(2,1)S(1)}, bf16[256,512]{1,0:T(8,128)(2,1)S(1)}, u32[]{:S(2)}, u32[]{:S(2)}) collective-permute-start(bf16[256,512]{1,0:T(8,128)(2,1)S(1)} %pad_maximum_fusion.5), channel_id=1, source_target_pairs={{0,2},{1,3},{2,4},{3,5},{4,6},{5,7},{8,10},{9,11},{10,12},{11,13},... | collective-permute-start | bytes 786440 | tf_op jit(solution)/shard_map/ppermute | solution.py:24
  28.3 3.5 %collective-permute-start.1 = (bf16[256,512]{0,1:T(8,128)(2,1)S(1)}, bf16[256,512]{0,1:T(8,128)(2,1)S(1)}, u32[]{:S(2)}, u32[]{:S(2)}) collective-permute-start(bf16[256,512]{0,1:T(8,128)(2,1)S(1)} %pad_maximum_fusion.4), channel_id=1, source_target_pairs={{0,2},{1,3},{2,4},{3,5},{4,6},{5,7},{8,10},{9,11},{10,12},{11,13},... | collective-permute-start | bytes 786440 | tf_op jit(solution)/shard_map/ppermute | solution.py:24
  31.8 2.5 %collective-permute-done.5 = bf16[256,512]{1,0:T(8,128)(2,1)S(1)} collective-permute-done((bf16[256,512]{1,0:T(8,128)(2,1)S(1)}, bf16[256,512]{1,0:T(8,128)(2,1)S(1)}, u32[]{:S(2)}, u32[]{:S(2)}) %collective-permute-start.5) | collective-permute-done | bytes 262176 | tf_op jit(solution)/shard_map/ppermute | solution.py:24
  35.1 2.3 %collective-permute-done.1 = bf16[256,512]{0,1:T(8,128)(2,1)S(1)} collective-permute-done((bf16[256,512]{0,1:T(8,128)(2,1)S(1)}, bf16[256,512]{0,1:T(8,128)(2,1)S(1)}, u32[]{:S(2)}, u32[]{:S(2)}) %collective-permute-start.1) | collective-permute-done | bytes 262176 | tf_op jit(solution)/shard_map/ppermute | solution.py:24
  46.5 0.8 copy.144
  47.3 0.8 copy.117
  48.8 0.8 copy.119
  50.4 0.8 copy.118
  53.6 1.3 %collective-permute-start.8 = (bf16[256,512]{0,1:T(8,128)(2,1)}, bf16[256,512]{0,1:T(8,128)(2,1)S(1)}, u32[]{:S(2)}, u32[]{:S(2)}) collective-permute-start(bf16[256,512]{0,1:T(8,128)(2,1)} %slice.180), channel_id=1, source_target_pairs={{2,0},{3,1},{4,2},{5,3},{6,4},{7,5},{10,8},{11,9},{12,10},{13,11},... | collective-permute-start | bytes 786440 | tf_op jit(solution)/shard_map/ppermute | solution.py:24
  54.9 1.3 %collective-permute-start.6 = (bf16[256,512]{0,1:T(8,128)(2,1)}, bf16[256,512]{0,1:T(8,128)(2,1)S(1)}, u32[]{:S(2)}, u32[]{:S(2)}) collective-permute-start(bf16[256,512]{0,1:T(8,128)(2,1)} %slice.181), channel_id=1, source_target_pairs={{2,0},{3,1},{4,2},{5,3},{6,4},{7,5},{10,8},{11,9},{12,10},{13,11},... | collective-permute-start | bytes 786440 | tf_op jit(solution)/shard_map/ppermute | solution.py:24
  56.3 1.1 maximum_bitcast_fusion
  57.4 42.7 %psum.7 = f32[16]{0:T(128)S(1)} all-reduce(f32[16]{0:T(128)S(1)} %pad_maximum_fusion.8), channel_id=1, replica_groups=mesh['dp'=4,'ctx'=8] {'dp','ctx'}, use_global_device_ids=true, to_apply=%region_19.20 | all-reduce | flops 16 | bytes 128 | tf_op jit(solution)/shard_map/psum | solution.py:162
  100.7 1.3 %collective-permute-start.9 = (bf16[128,512]{0,1:T(8,128)(2,1)S(1)}, bf16[128,512]{0,1:T(8,128)(2,1)S(1)}, u32[]{:S(2)}, u32[]{:S(2)}) collective-permute-start(bf16[128,512]{0,1:T(8,128)(2,1)S(1)} %slice.182), channel_id=1, source_target_pairs={{1,0},{2,1},{3,2},{4,3},{5,4},{6,5},{7,6},{9,8},{10,9},{11,10},{12... | collective-permute-start | bytes 393224 | tf_op jit(solution)/shard_map/ppermute | solution.py:24
  102.1 1.3 %collective-permute-start.7 = (bf16[128,512]{0,1:T(8,128)(2,1)S(1)}, bf16[128,512]{0,1:T(8,128)(2,1)S(1)}, u32[]{:S(2)}, u32[]{:S(2)}) collective-permute-start(bf16[128,512]{0,1:T(8,128)(2,1)S(1)} %slice.183), channel_id=1, source_target_pairs={{1,0},{2,1},{3,2},{4,3},{5,4},{6,5},{7,6},{9,8},{10,9},{11,10},{12... | collective-permute-start | bytes 393224 | tf_op jit(solution)/shard_map/ppermute | solution.py:24
  103.4 5.6 %collective-permute-done.9 = bf16[128,512]{0,1:T(8,128)(2,1)S(1)} collective-permute-done((bf16[128,512]{0,1:T(8,128)(2,1)S(1)}, bf16[128,512]{0,1:T(8,128)(2,1)S(1)}, u32[]{:S(2)}, u32[]{:S(2)}) %collective-permute-start.9) | collective-permute-done | bytes 131104 | tf_op jit(solution)/shard_map/ppermute | solution.py:24
  109.1 0.8 copy.154
  110.5 0.8 copy.153
  (112 shorter events, 19.7 us)
Async XLA Ops:
  1.3 9.5 %copy-start.8 = (bf16[1,128,512]{2,1,0:T(8,128)(2,1)S(1)}, bf16[1,128,512]{2,1,0:T(8,128)(2,1)}, u32[]{:S(2)}) copy-start(bf16[1,128,512]{2,1,0:T(8,128)(2,1)} %param.8) | copy-start | bytes 393220
  1.3 17.7 %collective-permute-start.2 = (bf16[128]{0:T(256)(128)(2,1)S(1)}, bf16[128]{0:T(256)(128)(2,1)S(1)}, u32[]{:S(2)}, u32[]{:S(2)}) collective-permute-start(bf16[128]{0:T(256)(128)(2,1)S(1)} %convert_bitcast_fusion), channel_id=1, source_target_pairs={{0,1},{1,2},{2,3},{3,4},{4,5},{5,6},{6,7},{8,9},{9,10},{10,11},{11... | collective-permute-start | bytes 776 | tf_op jit(solution)/shard_map/ppermute | solution.py:24
  7.3 20.9 %collective-permute-start = (bf16[128,512]{0,1:T(8,128)(2,1)S(1)}, bf16[128,512]{0,1:T(8,128)(2,1)S(1)}, u32[]{:S(2)}, u32[]{:S(2)}) collective-permute-start(bf16[128,512]{0,1:T(8,128)(2,1)S(1)} %bitcast.233), channel_id=1, source_target_pairs={{0,1},{1,2},{2,3},{3,4},{4,5},{5,6},{6,7},{8,9},{9,10},{10,11},{11... | collective-permute-start | bytes 393224 | tf_op jit(solution)/shard_map/ppermute | solution.py:24
  10.8 13.0 %collective-permute-start.4 = (bf16[128,512]{1,0:T(8,128)(2,1)S(1)}, bf16[128,512]{1,0:T(8,128)(2,1)S(1)}, u32[]{:S(2)}, u32[]{:S(2)}) collective-permute-start(bf16[128,512]{1,0:T(8,128)(2,1)S(1)} %bitcast.253), channel_id=1, source_target_pairs={{0,1},{1,2},{2,3},{3,4},{4,5},{5,6},{6,7},{8,9},{9,10},{10,11},{11... | collective-permute-start | bytes 393224 | tf_op jit(solution)/shard_map/ppermute | solution.py:24
  14.2 0.7 copy-start.10
  15.0 0.7 copy-start.9
  17.1 1.0 copy-start.7
  19.0 4.8 %collective-permute-start.3 = (bf16[256]{0:T(256)(128)(2,1)S(1)}, bf16[256]{0:T(256)(128)(2,1)S(1)}, u32[]{:S(2)}, u32[]{:S(2)}) collective-permute-start(bf16[256]{0:T(256)(128)(2,1)S(1)} %pad_maximum_fusion.7), channel_id=1, source_target_pairs={{0,2},{1,3},{2,4},{3,5},{4,6},{5,7},{8,10},{9,11},{10,12},{11,13},... | collective-permute-start | bytes 1544 | tf_op jit(solution)/shard_map/ppermute | solution.py:24
  23.8 10.5 %collective-permute-start.5 = (bf16[256,512]{1,0:T(8,128)(2,1)S(1)}, bf16[256,512]{1,0:T(8,128)(2,1)S(1)}, u32[]{:S(2)}, u32[]{:S(2)}) collective-permute-start(bf16[256,512]{1,0:T(8,128)(2,1)S(1)} %pad_maximum_fusion.5), channel_id=1, source_target_pairs={{0,2},{1,3},{2,4},{3,5},{4,6},{5,7},{8,10},{9,11},{10,12},{11,13},... | collective-permute-start | bytes 786440 | tf_op jit(solution)/shard_map/ppermute | solution.py:24
  28.3 9.1 %collective-permute-start.1 = (bf16[256,512]{0,1:T(8,128)(2,1)S(1)}, bf16[256,512]{0,1:T(8,128)(2,1)S(1)}, u32[]{:S(2)}, u32[]{:S(2)}) collective-permute-start(bf16[256,512]{0,1:T(8,128)(2,1)S(1)} %pad_maximum_fusion.4), channel_id=1, source_target_pairs={{0,2},{1,3},{2,4},{3,5},{4,6},{5,7},{8,10},{9,11},{10,12},{11,13},... | collective-permute-start | bytes 786440 | tf_op jit(solution)/shard_map/ppermute | solution.py:24
  52.7 3.5 %copy-start.4 = (bf16[128,512]{1,0:T(8,128)(2,1)S(1)}, bf16[128,512]{1,0:T(8,128)(2,1)}, u32[]{:S(2)}) copy-start(bf16[128,512]{1,0:T(8,128)(2,1)} %copy.143) | copy-start | bytes 393220
  52.7 3.5 %copy-start.5 = (bf16[128,512]{1,0:T(8,128)(2,1)S(1)}, bf16[128,512]{1,0:T(8,128)(2,1)}, u32[]{:S(2)}) copy-start(bf16[128,512]{1,0:T(8,128)(2,1)} %copy.118) | copy-start | bytes 393220
  52.7 3.5 %copy-start.6 = (bf16[128,512]{1,0:T(8,128)(2,1)S(1)}, bf16[128,512]{1,0:T(8,128)(2,1)}, u32[]{:S(2)}) copy-start(bf16[128,512]{1,0:T(8,128)(2,1)} %copy.142) | copy-start | bytes 393220
  52.8 3.5 %copy-start = (bf16[128,512]{1,0:T(8,128)(2,1)S(1)}, bf16[128,512]{1,0:T(8,128)(2,1)}, u32[]{:S(2)}) copy-start(bf16[128,512]{1,0:T(8,128)(2,1)} %copy.144) | copy-start | bytes 393220
  52.8 3.5 %copy-start.1 = (bf16[128,512]{1,0:T(8,128)(2,1)S(1)}, bf16[128,512]{1,0:T(8,128)(2,1)}, u32[]{:S(2)}) copy-start(bf16[128,512]{1,0:T(8,128)(2,1)} %copy.117) | copy-start | bytes 393220
  52.8 3.5 %copy-start.2 = (bf16[128,512]{1,0:T(8,128)(2,1)S(1)}, bf16[128,512]{1,0:T(8,128)(2,1)}, u32[]{:S(2)}) copy-start(bf16[128,512]{1,0:T(8,128)(2,1)} %copy.141) | copy-start | bytes 393220
  52.8 3.5 %copy-start.3 = (bf16[128,512]{1,0:T(8,128)(2,1)S(1)}, bf16[128,512]{1,0:T(8,128)(2,1)}, u32[]{:S(2)}) copy-start(bf16[128,512]{1,0:T(8,128)(2,1)} %copy.119) | copy-start | bytes 393220
  53.6 47.0 %collective-permute-start.8 = (bf16[256,512]{0,1:T(8,128)(2,1)}, bf16[256,512]{0,1:T(8,128)(2,1)S(1)}, u32[]{:S(2)}, u32[]{:S(2)}) collective-permute-start(bf16[256,512]{0,1:T(8,128)(2,1)} %slice.180), channel_id=1, source_target_pairs={{2,0},{3,1},{4,2},{5,3},{6,4},{7,5},{10,8},{11,9},{12,10},{13,11},... | collective-permute-start | bytes 786440 | tf_op jit(solution)/shard_map/ppermute | solution.py:24
  54.9 47.2 %collective-permute-start.6 = (bf16[256,512]{0,1:T(8,128)(2,1)}, bf16[256,512]{0,1:T(8,128)(2,1)S(1)}, u32[]{:S(2)}, u32[]{:S(2)}) collective-permute-start(bf16[256,512]{0,1:T(8,128)(2,1)} %slice.181), channel_id=1, source_target_pairs={{2,0},{3,1},{4,2},{5,3},{6,4},{7,5},{10,8},{11,9},{12,10},{13,11},... | collective-permute-start | bytes 786440 | tf_op jit(solution)/shard_map/ppermute | solution.py:24
  100.7 8.4 %collective-permute-start.9 = (bf16[128,512]{0,1:T(8,128)(2,1)S(1)}, bf16[128,512]{0,1:T(8,128)(2,1)S(1)}, u32[]{:S(2)}, u32[]{:S(2)}) collective-permute-start(bf16[128,512]{0,1:T(8,128)(2,1)S(1)} %slice.182), channel_id=1, source_target_pairs={{1,0},{2,1},{3,2},{4,3},{5,4},{6,5},{7,6},{9,8},{10,9},{11,10},{12... | collective-permute-start | bytes 393224 | tf_op jit(solution)/shard_map/ppermute | solution.py:24
  102.1 8.4 %collective-permute-start.7 = (bf16[128,512]{0,1:T(8,128)(2,1)S(1)}, bf16[128,512]{0,1:T(8,128)(2,1)S(1)}, u32[]{:S(2)}, u32[]{:S(2)}) collective-permute-start(bf16[128,512]{0,1:T(8,128)(2,1)S(1)} %slice.183), channel_id=1, source_target_pairs={{1,0},{2,1},{3,2},{4,3},{5,4},{6,5},{7,6},{9,8},{10,9},{11,10},{12... | collective-permute-start | bytes 393224 | tf_op jit(solution)/shard_map/ppermute | solution.py:24
where the time goes:
time: 112 us; the launch traced here: 111 us
  blocking collectives  42.7 us (38%)
  starting transfers between devices  28.1 us (25%)
  local copies, waits for them, and re-layouts  13.2 us (12%)
  waiting for transfers between devices  11.8 us (11%)
  other arithmetic  7.14 us (6%)
  matrix products  7.11 us (6%)
  between operations  1.2 us (1%)
    psum x1, blocking collectives, body(): sink_total = lax.psum(grad_sink, ('dp', 'ctx'))  42.7 us
    ppermute x10, starting transfers between devices, passed_along(): return lax.ppermute(array, axis, pairs)  28.1 us
    ppermute x10, waiting for transfers between devices, passed_along(): return lax.ppermute(array, axis, pairs)  11.8 us
    unnamed x26, local copies, waits for them, and re-layouts  5.57 us
    reshape x8, local copies, waits for them, and re-layouts, window_work(): block_out.reshape(tok_rows, -1)  5.47 us
  transfers between devices with their start and end apart: 10, of which 5 were waited for; matrix products, arithmetic and copies ran while one was open for 8% of the time, Pallas kernels for 0%

commit v1 on v0

v1 whole, which is shorter than its diff:
```python
import functools
import math

import jax
import jax.numpy as jnp
from jax import lax
from jax.experimental import pallas as pl
from jax.experimental.pallas import tpu as pltpu
from jax.sharding import PartitionSpec as P

HEADS = 16
KV_HEADS = 4
HEAD_DIM = 128
GROUP = HEADS // KV_HEADS
LOG2E = math.log2(math.e)
AWAY = -1e30
MESH = pl.DeviceIdType.MESH


def edge_lists(most):
    edges = {0: [], 1: []}
    for parity in (0, 1):
        for kept in range(1, most):
            if parity == 0:
                step = -1 if kept == 1 and most > 2 else min(kept, 2)
            else:
                step = {1: 1, 2: 2, 3: 1}.get(kept, 2)
            sender = parity if step % 2 == 0 else 1 - parity
            edges[sender].append((kept - step, step, kept))
    return edges


def levels(edges, most):
    depth = {(0, 0): 0, (1, 0): 0}
    while len(depth) < 2 * most:
        for parity in (0, 1):
            for held, step, kept in edges[parity]:
                if (parity, held) in depth:
                    depth[((parity + step) % 2, kept)] = depth[(parity, held)] + 1
    return depth


def kernel(
    n_dp, n_ctx, most,
    sink_ref, runs_ref, q_ref, k_ref, v_ref, do_ref, seg_ref,
    att_ref, dq_ref, dk_ref, dv_ref, dsink_ref,
    kv, gsum, gout, gin, segs, bias, sink_rows, ctx_rows, dp_rows,
    f_send, f_recv, b_send, b_recv, s_send, s_recv, c_send, c_recv, d_send, d_recv,
):
    tok = k_ref.shape[1]
    me = lax.axis_index("ctx")
    my_dp = lax.axis_index("dp")
    odd = lax.rem(me, 2)
    edges = edge_lists(most)
    depth = levels(edges, most)
    deepest = max(depth.values())
    factor = HEAD_DIM ** (-0.5)

    barrier = pltpu.get_barrier_semaphore()
    for j in range(1, n_ctx):
        pl.semaphore_signal(barrier, inc=1, device_id={"ctx": lax.rem(me + j, n_ctx)}, device_id_type=MESH)
    for j in range(1, n_dp):
        pl.semaphore_signal(barrier, inc=1, device_id={"dp": lax.rem(my_dp + j, n_dp)}, device_id_type=MESH)
    for h in range(KV_HEADS):
        cols = slice(h * HEAD_DIM, (h + 1) * HEAD_DIM)
        kv[h, 0, 0:tok, :] = k_ref[0, :, cols]
        kv[h, 1, 0:tok, :] = v_ref[0, :, cols]
    segs[0] = seg_ref[...]
    pl.semaphore_wait(barrier, n_ctx - 1 + n_dp - 1)

    def rows(dist):
        return pl.ds(dist * tok, tok)

    def forward(h, parity, index):
        held, step, kept = edges[parity][index]
        return pltpu.make_async_remote_copy(
            src_ref=kv.at[h, :, rows(held)],
            dst_ref=kv.at[h, :, rows(kept)],
            send_sem=f_send.at[h, index],
            recv_sem=f_recv.at[h, kept],
            device_id={"ctx": me + step},
            device_id_type=MESH,
        )

    def backward(h, kept, parity, index):
        held, step, k = edges[parity][index]
        return pltpu.make_async_remote_copy(
            src_ref=gout.at[h, :, rows(kept)],
            dst_ref=gin.at[h, index],
            send_sem=b_send.at[h, kept],
            recv_sem=b_recv.at[h, index],
            device_id={"ctx": me - step},
            device_id_type=MESH,
        )

    def edge_live(held, step):
        return (me >= held) & (me + step >= 0) & (me + step < n_ctx)

    def start_forward(h, level):
        for parity in (0, 1):
            for index, (held, step, kept) in enumerate(edges[parity]):
                if depth[(parity, held)] == level:
                    @pl.when((odd == parity) & edge_live(held, step))
                    def _():
                        forward(h, parity, index).start()

    def wait_forward(h, level):
        for kept in range(1, most):
            for parity in (0, 1):
                if depth[(parity, kept)] == level:
                    @pl.when((odd == parity) & (me >= kept))
                    def _():
                        pltpu.make_async_remote_copy(
                            src_ref=kv.at[h, :, rows(kept)],
                            dst_ref=kv.at[h, :, rows(kept)],
                            send_sem=f_send.at[h, 0],
                            recv_sem=f_recv.at[h, kept],
                            device_id={"ctx": lax.rem(me + 1, n_ctx)},
                            device_id_type=MESH,
                        ).wait_recv()

    def parent_edge(parity, kept):
        for p in (0, 1):
            for index, (held, step, k) in enumerate(edges[p]):
                if k == kept and (p + step) % 2 == parity:
                    return p, index

    def child_level(parity, held):
        below = [
            child_level((parity + step) % 2, kept) + 1
            for h0, step, kept in edges[parity] if h0 == held
        ]
        return max(below, default=0)

    def back_step(h, level):
        for parity in (0, 1):
            for held in range(most):
                if child_level(parity, held) != level:
                    continue
                for index, (h0, step, kept) in enumerate(edges[parity]):
                    if h0 == held:
                        @pl.when((odd == parity) & edge_live(held, step))
                        def _():
                            pltpu.make_async_remote_copy(
                                src_ref=gin.at[h, index],
                                dst_ref=gin.at[h, index],
                                send_sem=b_send.at[h, 0],
                                recv_sem=b_recv.at[h, index],
                                device_id={"ctx": lax.rem(me + 1, n_ctx)},
                                device_id_type=MESH,
                            ).wait_recv()
                            gsum[h, :, rows(held)] += gin[h, index].astype(jnp.float32)
                if held == 0:
                    @pl.when(odd == parity)
                    def _():
                        cols = slice(h * HEAD_DIM, (h + 1) * HEAD_DIM)
                        dk_ref[0, :, cols] = gsum[h, 0, 0:tok].astype(dk_ref.dtype)
                        dv_ref[0, :, cols] = gsum[h, 1, 0:tok].astype(dv_ref.dtype)
                else:
                    p, index = parent_edge(parity, held)
                    @pl.when((odd == parity) & (me >= held))
                    def _():
                        gout[h, :, rows(held)] = gsum[h, :, rows(held)].astype(gout.dtype)
                        backward(h, held, p, index).start()

    def seg_copy(dist):
        return pltpu.make_async_remote_copy(
            src_ref=segs.at[0], dst_ref=segs.at[dist],
            send_sem=s_send.at[dist], recv_sem=s_recv.at[dist],
            device_id={"ctx": me + dist}, device_id_type=MESH,
        )

    for dist in range(1, most):
        @pl.when(me + dist < n_ctx)
        def _():
            seg_copy(dist).start()
    for h in range(KV_HEADS):
        start_forward(h, 0)

    for dist in range(1, most):
        @pl.when(me < dist)
        def _():
            kv[:, :, rows(dist), :] = jnp.zeros((KV_HEADS, 2, tok, HEAD_DIM), kv.dtype)
            segs[dist] = jnp.full(segs.shape[1:], -1, segs.dtype)

    for dist in range(1, most):
        @pl.when(me >= dist)
        def _():
            seg_copy(dist).wait_recv()

    def traj(shard):
        end, count = 0, 0
        for i in range(runs_ref.shape[1]):
            end = end + runs_ref[0, i]
            count = count + jnp.where(end <= shard, 1, 0)
        return count

    mine = traj(me)
    seg_query = jnp.broadcast_to(segs[0], (tok, tok))
    for dist in range(most):
        seg_key = jnp.transpose(jnp.broadcast_to(segs[dist], (tok, tok)).astype(jnp.float32))
        level = jnp.where((traj(me - dist) == mine) & (me >= dist), 0.0, AWAY)
        allowed = seg_key == seg_query.astype(jnp.float32)
        if dist == 0:
            key_pos = lax.broadcasted_iota(jnp.int32, (tok, tok), 0)
            query_pos = lax.broadcasted_iota(jnp.int32, (tok, tok), 1)
            allowed = allowed & (key_pos <= query_pos)
        bias[rows(dist), :] = jnp.where(allowed, level, AWAY)

    def nn(a, b):
        return jnp.dot(a, b, preferred_element_type=jnp.float32)

    def compute(h):
        heads = [h * GROUP + g for g in range(GROUP)]
        keys, values = kv[h, 0], kv[h, 1]
        keys_t, values_t = keys.T, values.T
        gk = gv = None
        for g in range(GROUP):
            cols = slice(heads[g] * HEAD_DIM, (heads[g] + 1) * HEAD_DIM)
            q = q_ref[0, :, cols]
            do = do_ref[0, :, cols]
            do_t = do.T
            scores = nn(keys, q.T) * (factor * LOG2E) + bias[...]
            sink = sink_ref[heads[g]] * LOG2E
            top = jnp.maximum(jnp.max(scores, axis=0, keepdims=True), sink)
            terms = jnp.exp2(scores - top)
            sink_exp = jnp.exp2(sink - top)
            denom = jnp.sum(terms, axis=0, keepdims=True) + sink_exp
            inv = 1.0 / denom
            weights = terms * inv
            low = weights.astype(jnp.bfloat16)
            att = nn(values_t, low).astype(jnp.bfloat16)
            att_ref[0, :, cols] = att.T
            row_dot = jnp.sum(att.astype(jnp.float32) * do_t.astype(jnp.float32), axis=0, keepdims=True)
            gw = nn(values, do_t)
            gs = (weights * (gw - row_dot)).astype(jnp.bfloat16)
            gq = nn(keys_t, gs) * factor
            dq_ref[0, :, cols] = gq.astype(jnp.bfloat16).T
            new_k, new_v = nn(gs, q), nn(low, do)
            gk = new_k if gk is None else gk + new_k
            gv = new_v if gv is None else gv + new_v
            sink_rows[pl.ds(heads[g], 1), :] = -(sink_exp * inv * row_dot)
        gsum[h, 0] = gk * factor
        gsum[h, 1] = gv

    def run_forward(upto):
        for h, level in upto:
            wait_forward(h, level)
            if level < deepest:
                start_forward(h, level)

    order = sorted(
        ((h, level) for h in range(KV_HEADS) for level in range(1, deepest + 1)),
        key=lambda item: (item[0] + item[1], item[0]),
    )
    done = 0
    back_deepest = max(child_level(p, k) for p in (0, 1) for k in range(most))
    pending = []
    for h in range(KV_HEADS):
        last = order.index((h, deepest)) + 1
        run_forward(order[done:last])
        done = max(done, last)
        compute(h)
        back_step(h, 0)
        for other in range(h):
            level = h - other
            if level <= back_deepest:
                back_step(other, level)
                pending.append((other, level))

    padded = jnp.concatenate(
        [sink_rows[...], jnp.zeros((128 - HEADS, tok), jnp.float32)], 0
    )
    ctx_rows[me] = jnp.sum(padded.T, axis=0, keepdims=True)

    def ctx_copy(j):
        return pltpu.make_async_remote_copy(
            src_ref=ctx_rows.at[me], dst_ref=ctx_rows.at[me],
            send_sem=c_send.at[j], recv_sem=c_recv.at[me],
            device_id={"ctx": lax.rem(me + j, n_ctx)}, device_id_type=MESH,
        )

    def dp_copy(j):
        return pltpu.make_async_remote_copy(
            src_ref=dp_rows.at[my_dp], dst_ref=dp_rows.at[my_dp],
            send_sem=d_send.at[j], recv_sem=d_recv.at[my_dp],
            device_id={"dp": lax.rem(my_dp + j, n_dp)}, device_id_type=MESH,
        )

    for j in range(1, n_ctx):
        ctx_copy(j).start()

    rest = sorted(
        ((h, level) for h in range(KV_HEADS) for level in range(1, back_deepest + 1)
         if (h, level) not in pending),
        key=lambda item: (item[0] + item[1], item[0]),
    )
    half = [item for item in rest if item != (KV_HEADS - 1, back_deepest)]
    for h, level in half:
        back_step(h, level)

    for j in range(1, n_ctx):
        other = lax.rem(me + j, n_ctx)
        pltpu.make_async_remote_copy(
            src_ref=ctx_rows.at[other], dst_ref=ctx_rows.at[other],
            send_sem=c_send.at[j], recv_sem=c_recv.at[other],
            device_id={"ctx": other}, device_id_type=MESH,
        ).wait_recv()
    total = ctx_rows[0]
    for j in range(1, n_ctx):
        total = total + ctx_rows[j]
    dp_rows[my_dp] = total
    for j in range(1, n_dp):
        dp_copy(j).start()

    for item in rest:
        if item not in half:
            back_step(*item)

    for j in range(1, n_dp):
        other = lax.rem(my_dp + j, n_dp)
        pltpu.make_async_remote_copy(
            src_ref=dp_rows.at[other], dst_ref=dp_rows.at[other],
            send_sem=d_send.at[j], recv_sem=d_recv.at[other],
            device_id={"dp": other}, device_id_type=MESH,
        ).wait_recv()
    total = dp_rows[0]
    for j in range(1, n_dp):
        total = total + dp_rows[j]
    dsink_ref[...] = total * (1.0 / math.sqrt(n_dp * n_ctx * tok))

    for dist in range(1, most):
        @pl.when(me + dist < n_ctx)
        def _():
            seg_copy(dist).wait_send()
    for h in range(KV_HEADS):
        for parity in (0, 1):
            for index, (held, step, kept) in enumerate(edges[parity]):
                @pl.when((odd == parity) & edge_live(held, step))
                def _():
                    forward(h, parity, index).wait_send()
            for held in range(1, most):
                p, index = parent_edge(parity, held)
                @pl.when((odd == parity) & (me >= held))
                def _():
                    backward(h, held, p, index).wait_send()
    for j in range(1, n_ctx):
        ctx_copy(j).wait_send()
    for j in range(1, n_dp):
        dp_copy(j).wait_send()


def body(n_dp, n_ctx, queries, key_rows, value_rows, cotangent, sink_logits, run_lengths, segment_ids):
    tok = queries.shape[1]
    most = min(8, n_ctx // 2)
    n_edges = max(len(part) for part in edge_lists(most).values())
    span = most * tok
    vmem = pl.BlockSpec(memory_space=pltpu.VMEM)
    smem = pl.BlockSpec(memory_space=pltpu.SMEM)
    like = lambda array: jax.ShapeDtypeStruct(array.shape, array.dtype)
    dma = pltpu.SemaphoreType.DMA
    flops = 12 * HEADS * tok * span * HEAD_DIM
    outs = pl.pallas_call(
        functools.partial(kernel, n_dp, n_ctx, most),
        out_shape=(
            like(queries), like(queries), like(key_rows), like(value_rows),
            jax.ShapeDtypeStruct((1, 128), jnp.float32),
        ),
        in_specs=[smem, smem] + [vmem] * 5,
        out_specs=[vmem] * 5,
        scratch_shapes=[
            pltpu.VMEM((KV_HEADS, 2, span, HEAD_DIM), jnp.bfloat16),
            pltpu.VMEM((KV_HEADS, 2, span, HEAD_DIM), jnp.float32),
            pltpu.VMEM((KV_HEADS, 2, span, HEAD_DIM), jnp.bfloat16),
            pltpu.VMEM((KV_HEADS, n_edges, 2, tok, HEAD_DIM), jnp.bfloat16),
            pltpu.VMEM((most, 1, tok), jnp.int32),
            pltpu.VMEM((span, tok), jnp.float32),
            pltpu.VMEM((HEADS, tok), jnp.float32),
            pltpu.VMEM((n_ctx, 1, 128), jnp.float32),
            pltpu.VMEM((n_dp, 1, 128), jnp.float32),
            dma((KV_HEADS, n_edges)), dma((KV_HEADS, most)),
            dma((KV_HEADS, most)), dma((KV_HEADS, n_edges)),
            dma((most,)), dma((most,)),
            dma((n_ctx,)), dma((n_ctx,)), dma((n_dp,)), dma((n_dp,)),
        ],
        compiler_params=pltpu.CompilerParams(
            collective_id=0, has_side_effects=True, vmem_limit_bytes=48 * 1024 * 1024
        ),
        cost_estimate=pl.CostEstimate(
            flops=flops, bytes_accessed=5 * tok * HEADS * HEAD_DIM * 2, transcendentals=HEADS * tok * span
        ),
    )(sink_logits, run_lengths, queries, key_rows, value_rows, cotangent, segment_ids)
    return (*outs[:4], outs[4][0, :HEADS])


def solution(mesh):
    rows = P("dp", "ctx", None)
    return jax.shard_map(
        functools.partial(body, mesh.shape["dp"], mesh.shape["ctx"]),
        mesh=mesh,
        in_specs=(rows, rows, rows, rows, P(), P("dp", None), P("dp", "ctx")),
        out_specs=(rows, rows, rows, rows, P()),
        check_vma=False,
    )
```

time: 112 us -> 57.7 us (0.52)
  Pallas kernels: 0 us -> 47.5 us
  blocking collectives: 42.7 us -> 0 us
  starting transfers between devices: 28.1 us -> 0 us
  waiting for transfers between devices: 11.8 us -> 0 us
  other arithmetic: 7.14 us -> 0 us
  matrix products: 7.11 us -> 0 us
  local copies, waits for them, and re-layouts: 13.2 us -> 9.26 us
    pallas_call x0 -> x1, Pallas kernels: none -> 47.5 us  [body(): pl.pallas_call(functools.partial(kernel, n_dp, n_ctx, most), out_shape=(l...]
    psum x1 -> x0, blocking collectives: 42.7 us -> none  [body(): sink_total = lax.psum(grad_sink, ('dp', 'ctx'))]
    ppermute x10 -> x0, starting transfers between devices: 28.1 us -> none  [passed_along(): return lax.ppermute(array, axis, pairs)]
    ppermute x10 -> x0, waiting for transfers between devices: 11.8 us -> none  [passed_along(): return lax.ppermute(array, axis, pairs)]
    dot_general x24 -> x0, matrix products: 7.11 us -> none  [the longest x4 1.5 us: head_block(): jnp.einsum('rgd,wd->grw', grad_heads, value_win, preferred_element_type=j...]
    reshape x8 -> x0, local copies, waits for them, and re-layouts: 5.47 us -> none  [window_work(): block_out.reshape(tok_rows, -1)]
    unnamed x26 -> x18, local copies, waits for them, and re-layouts: 5.57 us -> 8.74 us
    slice x11 -> x0, local copies, waits for them, and re-layouts: 2.13 us -> none  [the longest x2 0.76 us: body(): padded[1][:split_row].astype(jnp.bfloat16)]
  transfers between devices with their start and end apart: 10 -> 0, of which waited for: 5 -> 0; matrix products, arithmetic and copies ran while one was open for 8% -> 0% of each run, Pallas kernels for 0% -> 0%
where the time goes in v1:
time: 57.7 us; the launch traced here: 57.4 us
  Pallas kernels  47.5 us (82%)
  local copies, waits for them, and re-layouts  9.26 us (16%)
  between operations  0.66 us (1%)
    pallas_call x1, Pallas kernels, body(): pl.pallas_call(functools.partial(kernel, n_dp, n_ctx, most), out_shape=(l...  47.5 us
    unnamed x18, local copies, waits for them, and re-layouts  8.74 us

profile of v1, /device:TPU:0, one launch (start us, length us, event | category | flops | bytes accessed | tf_op | source)
XLA Modules:
  0.0 57.4 jit_solution(10352237116942267250)
XLA Ops:
  0.6 0.0 copy-start
  0.6 1.0 %copy-done = bf16[1,128,2048]{2,1,0:T(8,128)(2,1)S(1)} copy-done((bf16[1,128,2048]{2,1,0:T(8,128)(2,1)S(1)}, bf16[1,128,2048]{2,1,0:T(8,128)(2,1)}, u32[]{:S(2)}) %copy-start) | copy-done | bytes 524312
  1.7 0.0 copy-start.1
  1.7 1.0 %copy-done.1 = bf16[1,128,2048]{2,1,0:T(8,128)(2,1)S(1)} copy-done((bf16[1,128,2048]{2,1,0:T(8,128)(2,1)S(1)}, bf16[1,128,2048]{2,1,0:T(8,128)(2,1)}, u32[]{:S(2)}) %copy-start.1) | copy-done | bytes 524312
  2.7 0.0 copy-start.2
  2.7 0.9 %copy-done.2 = bf16[1,128,512]{2,1,0:T(8,128)(2,1)S(1)} copy-done((bf16[1,128,512]{2,1,0:T(8,128)(2,1)S(1)}, bf16[1,128,512]{2,1,0:T(8,128)(2,1)}, u32[]{:S(2)}) %copy-start.2) | copy-done | bytes 131096
  3.6 0.0 copy-start.3
  3.6 0.9 %copy-done.3 = bf16[1,128,512]{2,1,0:T(8,128)(2,1)S(1)} copy-done((bf16[1,128,512]{2,1,0:T(8,128)(2,1)S(1)}, bf16[1,128,512]{2,1,0:T(8,128)(2,1)}, u32[]{:S(2)}) %copy-start.3) | copy-done | bytes 131096
  4.5 0.0 copy-start.4
  4.5 0.7 %copy-done.4 = f32[16]{0:T(128)S(1)} copy-done((f32[16]{0:T(128)S(1)}, f32[16]{0:T(128)}, u32[]{:S(2)}) %copy-start.4) | copy-done | bytes 88
  5.2 0.0 copy-start.5
  5.2 0.7 %copy-done.5 = s32[1,3]{1,0:T(1,128)S(1)} copy-done((s32[1,3]{1,0:T(1,128)S(1)}, s32[1,3]{1,0:T(1,128)}, u32[]{:S(2)}) %copy-start.5) | copy-done | bytes 36
  5.8 0.0 copy-start.6
  5.8 0.7 %copy-done.6 = s32[1,128]{1,0:T(1,128)S(1)} copy-done((s32[1,128]{1,0:T(1,128)S(1)}, s32[1,128]{1,0:T(1,128)}, u32[]{:S(2)}) %copy-start.6) | copy-done | bytes 536
  6.5 47.5 %shard_map.110 = (bf16[1,128,2048]{2,1,0:T(8,128)(2,1)S(1)}, bf16[1,128,2048]{2,1,0:T(8,128)(2,1)S(1)}, bf16[1,128,512]{2,1,0:T(8,128)(2,1)S(1)}, bf16[1,128,512]{2,1,0:T(8,128)(2,1)S(1)}, f32[1,128]{1,0:T(1,128)S(1)}) custom-call(f32[16]{0:T(128)S(1)} %copy-done.4, s32[1,3]{1,0:T(1,128)S(1)} %copy-done.5, bf16[1,128,2048]{2,1,0:T(8,128)(2,1)S(1)} %copy-done, ...), custom_call_target="tpu_custom_call" | custom-call | flops 1610612736 | bytes 2621440 | tf_op jit(solution)/shard_map/pallas_call | solution.py:363
  54.0 0.5 slice_bitcast_fusion
  54.5 0.8 %copy.16 = bf16[1,128,2048]{2,1,0:T(8,128)(2,1)} copy(bf16[1,128,2048]{2,1,0:T(8,128)(2,1)S(1)} %get-tuple-element.20) | data formatting | bytes 1048576
  55.3 0.8 %copy.17 = bf16[1,128,2048]{2,1,0:T(8,128)(2,1)} copy(bf16[1,128,2048]{2,1,0:T(8,128)(2,1)S(1)} %get-tuple-element.21) | data formatting | bytes 1048576
  56.1 0.7 %copy.18 = bf16[1,128,512]{2,1,0:T(8,128)(2,1)} copy(bf16[1,128,512]{2,1,0:T(8,128)(2,1)S(1)} %get-tuple-element.22) | data formatting | bytes 262144
  56.7 0.7 %copy.19 = bf16[1,128,512]{2,1,0:T(8,128)(2,1)} copy(bf16[1,128,512]{2,1,0:T(8,128)(2,1)S(1)} %get-tuple-element.23) | data formatting | bytes 262144
Async XLA Ops:
  0.6 1.0 %copy-start = (bf16[1,128,2048]{2,1,0:T(8,128)(2,1)S(1)}, bf16[1,128,2048]{2,1,0:T(8,128)(2,1)}, u32[]{:S(2)}) copy-start(bf16[1,128,2048]{2,1,0:T(8,128)(2,1)} %q_ref.1) | copy-start | bytes 1572868
  1.7 1.0 %copy-start.1 = (bf16[1,128,2048]{2,1,0:T(8,128)(2,1)S(1)}, bf16[1,128,2048]{2,1,0:T(8,128)(2,1)}, u32[]{:S(2)}) copy-start(bf16[1,128,2048]{2,1,0:T(8,128)(2,1)} %do_ref.1) | copy-start | bytes 1572868
  2.7 0.9 %copy-start.2 = (bf16[1,128,512]{2,1,0:T(8,128)(2,1)S(1)}, bf16[1,128,512]{2,1,0:T(8,128)(2,1)}, u32[]{:S(2)}) copy-start(bf16[1,128,512]{2,1,0:T(8,128)(2,1)} %k_ref.1) | copy-start | bytes 393220
  3.6 0.9 %copy-start.3 = (bf16[1,128,512]{2,1,0:T(8,128)(2,1)S(1)}, bf16[1,128,512]{2,1,0:T(8,128)(2,1)}, u32[]{:S(2)}) copy-start(bf16[1,128,512]{2,1,0:T(8,128)(2,1)} %v_ref.1) | copy-start | bytes 393220
  4.5 0.7 %copy-start.4 = (f32[16]{0:T(128)S(1)}, f32[16]{0:T(128)}, u32[]{:S(2)}) copy-start(f32[16]{0:T(128)} %sink_ref.1) | copy-start | bytes 196
  5.2 0.7 %copy-start.5 = (s32[1,3]{1,0:T(1,128)S(1)}, s32[1,3]{1,0:T(1,128)}, u32[]{:S(2)}) copy-start(s32[1,3]{1,0:T(1,128)} %runs_ref.1) | copy-start | bytes 40
  5.8 0.7 %copy-start.6 = (s32[1,128]{1,0:T(1,128)S(1)}, s32[1,128]{1,0:T(1,128)}, u32[]{:S(2)}) copy-start(s32[1,128]{1,0:T(1,128)} %seg_ref.1) | copy-start | bytes 1540

commit v2 on v1

--- a/solution.py
+++ b/solution.py
@@ -14,6 +14,8 @@
 GROUP = HEADS // KV_HEADS
 LOG2E = math.log2(math.e)
 AWAY = -1e30
+AHEAD = 4
+VMEM_BYTES = 64 * 1024 * 1024
 MESH = pl.DeviceIdType.MESH
 
 
@@ -21,10 +23,7 @@
     edges = {0: [], 1: []}
     for parity in (0, 1):
         for kept in range(1, most):
-            if parity == 0:
-                step = -1 if kept == 1 and most > 2 else min(kept, 2)
-            else:
-                step = {1: 1, 2: 2, 3: 1}.get(kept, 2)
+            step = 1 if kept == 1 or kept == 3 and parity == 1 else 2
             sender = parity if step % 2 == 0 else 1 - parity
             edges[sender].append((kept - step, step, kept))
     return edges
@@ -42,9 +41,10 @@
 
 def kernel(
     n_dp, n_ctx, most,
-    sink_ref, runs_ref, q_ref, k_ref, v_ref, do_ref, seg_ref,
+    sink_hbm, runs_hbm, q_hbm, k_ref, v_ref, do_hbm, seg_hbm,
     att_ref, dq_ref, dk_ref, dv_ref, dsink_ref,
     kv, gsum, gout, gin, segs, bias, sink_rows, ctx_rows, dp_rows,
+    q_ref, do_ref, sink_ref, runs_ref, i_sem, kv_sem,
     f_send, f_recv, b_send, b_recv, s_send, s_recv, c_send, c_recv, d_send, d_recv,
 ):
     tok = k_ref.shape[1]
@@ -61,11 +61,22 @@
         pl.semaphore_signal(barrier, inc=1, device_id={"ctx": lax.rem(me + j, n_ctx)}, device_id_type=MESH)
     for j in range(1, n_dp):
         pl.semaphore_signal(barrier, inc=1, device_id={"dp": lax.rem(my_dp + j, n_dp)}, device_id_type=MESH)
+    own = []
     for h in range(KV_HEADS):
-        cols = slice(h * HEAD_DIM, (h + 1) * HEAD_DIM)
-        kv[h, 0, 0:tok, :] = k_ref[0, :, cols]
-        kv[h, 1, 0:tok, :] = v_ref[0, :, cols]
-    segs[0] = seg_ref[...]
+        cols = pl.ds(h * HEAD_DIM, HEAD_DIM)
+        own.append([
+            pltpu.make_async_copy(ref.at[0, :, cols], kv.at[h, i, pl.ds(0, tok)], kv_sem.at[h, i])
+            for i, ref in enumerate((k_ref, v_ref))
+        ])
+    loads = [
+        pltpu.make_async_copy(source, target, i_sem.at[i])
+        for i, (source, target) in enumerate([
+            (seg_hbm, segs.at[0]), (runs_hbm, runs_ref), (sink_hbm, sink_ref),
+            (q_hbm, q_ref), (do_hbm, do_ref),
+        ])
+    ]
+    for copy in [loads[0]] + sum(own, []) + loads[1:]:
+        copy.start()
     pl.semaphore_wait(barrier, n_ctx - 1 + n_dp - 1)
 
     def rows(dist):
@@ -170,12 +181,21 @@
             device_id={"ctx": me + dist}, device_id_type=MESH,
         )
 
+    def start_own(h):
+        for copy in own[h]:
+            copy.wait()
+        start_forward(h, 0)
+
+    start_own(0)
+    loads[0].wait()
     for dist in range(1, most):
         @pl.when(me + dist < n_ctx)
         def _():
             seg_copy(dist).start()
-    for h in range(KV_HEADS):
-        start_forward(h, 0)
+    for h in range(1, AHEAD):
+        start_own(h)
+    for copy in loads[1:]:
+        copy.wait()
 
     for dist in range(1, most):
         @pl.when(me < dist)
@@ -248,6 +268,8 @@
             wait_forward(h, level)
             if level < deepest:
                 start_forward(h, level)
+            if level == 1 and h + AHEAD < KV_HEADS:
+                start_own(h + AHEAD)
 
     order = sorted(
         ((h, level) for h in range(KV_HEADS) for level in range(1, deepest + 1)),
@@ -257,7 +279,7 @@
     back_deepest = max(child_level(p, k) for p in (0, 1) for k in range(most))
     pending = []
     for h in range(KV_HEADS):
-        last = order.index((h, deepest)) + 1
+        last = sum(other + level <= h + deepest for other, level in order)
         run_forward(order[done:last])
         done = max(done, last)
         compute(h)
@@ -356,7 +378,7 @@
     n_edges = max(len(part) for part in edge_lists(most).values())
     span = most * tok
     vmem = pl.BlockSpec(memory_space=pltpu.VMEM)
-    smem = pl.BlockSpec(memory_space=pltpu.SMEM)
+    hbm = pl.BlockSpec(memory_space=pltpu.HBM)
     like = lambda array: jax.ShapeDtypeStruct(array.shape, array.dtype)
     dma = pltpu.SemaphoreType.DMA
     flops = 12 * HEADS * tok * span * HEAD_DIM
@@ -366,7 +388,7 @@
             like(queries), like(queries), like(key_rows), like(value_rows),
             jax.ShapeDtypeStruct((1, 128), jnp.float32),
         ),
-        in_specs=[smem, smem] + [vmem] * 5,
+        in_specs=[hbm] * 7,
         out_specs=[vmem] * 5,
         scratch_shapes=[
             pltpu.VMEM((KV_HEADS, 2, span, HEAD_DIM), jnp.bfloat16),
@@ -378,13 +400,16 @@
             pltpu.VMEM((HEADS, tok), jnp.float32),
             pltpu.VMEM((n_ctx, 1, 128), jnp.float32),
             pltpu.VMEM((n_dp, 1, 128), jnp.float32),
+            pltpu.VMEM(queries.shape, queries.dtype), pltpu.VMEM(cotangent.shape, cotangent.dtype),
+            pltpu.SMEM(sink_logits.shape, jnp.float32), pltpu.SMEM(run_lengths.shape, jnp.int32),
+            dma((5,)), dma((KV_HEADS, 2)),
             dma((KV_HEADS, n_edges)), dma((KV_HEADS, most)),
             dma((KV_HEADS, most)), dma((KV_HEADS, n_edges)),
             dma((most,)), dma((most,)),
             dma((n_ctx,)), dma((n_ctx,)), dma((n_dp,)), dma((n_dp,)),
         ],
         compiler_params=pltpu.CompilerParams(
-            collective_id=0, has_side_effects=True, vmem_limit_bytes=48 * 1024 * 1024
+            collective_id=0, has_side_effects=True, vmem_limit_bytes=VMEM_BYTES
         ),
         cost_estimate=pl.CostEstimate(
             flops=flops, bytes_accessed=5 * tok * HEADS * HEAD_DIM * 2, transcendentals=HEADS * tok * span

time: 57.7 us -> 48.9 us (0.85)
  Pallas kernels: 47.5 us -> 42.3 us
  local copies, waits for them, and re-layouts: 9.26 us -> 5.74 us
    pallas_call x1, Pallas kernels: 47.5 us -> 42.3 us  [body(): pl.pallas_call(functools.partial(kernel, n_dp, n_ctx, most), out_shape=(l...]
    unnamed x18 -> x12, local copies, waits for them, and re-layouts: 8.74 us -> 5.23 us
where the time goes in v2:
time: 48.9 us; the launch traced here: 48.7 us
  Pallas kernels  42.3 us (87%)
  local copies, waits for them, and re-layouts  5.74 us (12%)
  between operations  0.66 us (1%)
    pallas_call x1, Pallas kernels, body(): pl.pallas_call(functools.partial(kernel, n_dp, n_ctx, most), out_shape=(l...  42.3 us
    unnamed x12, local copies, waits for them, and re-layouts  5.23 us

profile of v2, /device:TPU:0, one launch (start us, length us, event | category | flops | bytes accessed | tf_op | source)
XLA Modules:
  0.0 48.7 jit_solution(13386282702012855216)
XLA Ops:
  0.6 42.3 %shard_map.110 = (bf16[1,128,2048]{2,1,0:T(8,128)(2,1)}, bf16[1,128,2048]{2,1,0:T(8,128)(2,1)}, bf16[1,128,512]{2,1,0:T(8,128)(2,1)}, bf16[1,128,512]{2,1,0:T(8,128)(2,1)}, f32[1,128]{1,0:T(1,128)}) custom-call(f32[16]{0:T(128)} %sink_hbm.1, s32[1,3]{1,0:T(1,128)} %runs_hbm.1, bf16[1,128,2048]{2,1,0:T(8,128)(2,1)} %q_hbm.1, bf16[1,128,512]{2,1,0:T(8,128)(2,1)} %k_ref.1, ...), custom_call_target="tpu_custom_call" | custom-call | flops 1610612736 | bytes 2621440 | tf_op jit(solution)/shard_map/pallas_call | solution.py:385
  43.0 0.0 copy-start.3
  43.0 0.7 %copy-done.3 = f32[1,128]{1,0:T(1,128)S(1)} copy-done((f32[1,128]{1,0:T(1,128)S(1)}, f32[1,128]{1,0:T(1,128)}, u32[]{:S(2)}) %copy-start.3) | copy-done | bytes 536
  43.6 0.5 %slice_bitcast_fusion = f32[16]{0:T(128)} fusion(f32[1,128]{1,0:T(1,128)S(1)} %copy-done.3), kind=kLoop, calls=%fused_computation | loop fusion | bytes 128 | tf_op jit(solution)/shard_map/squeeze | solution.py:418
  44.1 0.0 copy-start
  44.1 1.9 %copy.16 = bf16[1,128,2048]{2,1,0:T(8,128)(2,1)} copy(bf16[1,128,2048]{2,1,0:T(8,128)(2,1)} %get-tuple-element.20) | data formatting | bytes 1048576
  46.1 0.0 copy-done
  46.1 0.0 copy-start.2
  46.1 0.8 %copy.17 = bf16[1,128,2048]{2,1,0:T(8,128)(2,1)} copy(bf16[1,128,2048]{2,1,0:T(8,128)(2,1)S(1)} %copy-done) | data formatting | bytes 1048576
  46.9 0.2 copy-done.2
  47.1 0.0 copy-start.1
  47.1 0.7 %copy.18 = bf16[1,128,512]{2,1,0:T(8,128)(2,1)} copy(bf16[1,128,512]{2,1,0:T(8,128)(2,1)S(1)} %copy-done.2) | data formatting | bytes 262144
  47.8 0.3 copy-done.1
  48.1 0.7 %copy.19 = bf16[1,128,512]{2,1,0:T(8,128)(2,1)} copy(bf16[1,128,512]{2,1,0:T(8,128)(2,1)S(1)} %copy-done.1) | data formatting | bytes 262144
Async XLA Ops:
  43.0 0.7 %copy-start.3 = (f32[1,128]{1,0:T(1,128)S(1)}, f32[1,128]{1,0:T(1,128)}, u32[]{:S(2)}) copy-start(f32[1,128]{1,0:T(1,128)} %get-tuple-element.14) | copy-start | bytes 1540
  44.1 1.9 %copy-start = (bf16[1,128,2048]{2,1,0:T(8,128)(2,1)S(1)}, bf16[1,128,2048]{2,1,0:T(8,128)(2,1)}, u32[]{:S(2)}) copy-start(bf16[1,128,2048]{2,1,0:T(8,128)(2,1)} %get-tuple-element.21) | copy-start | bytes 1572868
  46.1 1.0 %copy-start.2 = (bf16[1,128,512]{2,1,0:T(8,128)(2,1)S(1)}, bf16[1,128,512]{2,1,0:T(8,128)(2,1)}, u32[]{:S(2)}) copy-start(bf16[1,128,512]{2,1,0:T(8,128)(2,1)} %get-tuple-element.22) | copy-start | bytes 393220
  47.1 1.0 %copy-start.1 = (bf16[1,128,512]{2,1,0:T(8,128)(2,1)S(1)}, bf16[1,128,512]{2,1,0:T(8,128)(2,1)}, u32[]{:S(2)}) copy-start(bf16[1,128,512]{2,1,0:T(8,128)(2,1)} %get-tuple-element.23) | copy-start | bytes 393220
